TPU v7x, 256 devices: a whole 4x4x8 slice. The times are simulated.
256 devices in a mesh: row: 8 (over x, y_hi), col: 32 (over z, y_lo, core).
Axes of the slice: x: 4, y: 4 (y_hi: 2, y_lo: 2; y = y_hi * 2 + y_lo), z: 8, core: 2. Of those that a mesh axis runs over, the one named last changes fastest.
Arguments:
- matrix: float32 [3, 8, 128, 32, 32, 128], P(None, 'row', None, None, 'col'), may hold values from -6 to 6
- factors: float32 [10, 512, 512], P(None, None, 'col'), as said below
- starts: int32 [10], replicated, may hold values from 0 to 2560, as said below
Outputs:
- updated: float32 [3, 8, 128, 32, 32, 128], P(None, 'row', None, None, 'col')
Inputs may be any that keep to these rules, and one draw needn't show every extreme that they name: starts[w] = starts[0] + 256 * w, and starts[0] is a multiple of 128. Each factors[w] is orthogonal.
All inputs are finite; a program needn't handle non-finite values.
Results may differ from a plain program's by a relative error of at most 0.0001.
Values sent between devices are 32-bit elements; how exact they have to be, the bound alone decides.
A program may use at most 128 MiB of HBM per device.

v0:
```python
import jax
import jax.numpy as jnp
from jax import lax
from jax.sharding import PartitionSpec as P

WIN = 512
SHIFT = 256
WINS = 10


def pick_tiles(first_tile, per_device, axis_count, position, span_tiles):
    global_tiles = (
        first_tile
        + jnp.remainder(position - first_tile, axis_count)
        + jnp.arange(per_device, dtype=jnp.int32) * axis_count
    )
    tile_valid = global_tiles < first_tile + span_tiles
    return (tile_valid, jnp.where(tile_valid, global_tiles // axis_count, 0))


def band_order(first_tile, axis_count, per_device, span_tiles):
    places = jnp.arange(span_tiles, dtype=jnp.int32)
    return jnp.remainder(first_tile + places, axis_count) * per_device + places // axis_count


def slot_order(first_tile, axis_count, per_device, span_tiles):
    slot_ids = jnp.arange(axis_count * per_device, dtype=jnp.int32)
    places = (
        jnp.remainder(slot_ids // per_device - first_tile, axis_count)
        + slot_ids % per_device * axis_count
    )
    slot_valid = places < span_tiles
    return (slot_valid, jnp.where(slot_valid, places, 0))


def body(matrix, factors, starts):
    row_count = lax.axis_size("row")
    col_count = lax.axis_size("col")
    row_place = lax.axis_index("row")
    col_place = lax.axis_index("col")
    row_cycles = matrix.shape[0]
    tile_size = matrix.shape[2]
    col_cycles = matrix.shape[3]
    span_tiles = (WIN + SHIFT * (WINS - 1)) // tile_size
    first_tile = starts[0] // tile_size
    all_factors = lax.all_gather(factors, "col", axis=2, tiled=True)

    def left_step(window, band_rows):
        offset_row = starts[window] - starts[0]
        factor_now = lax.dynamic_index_in_dim(all_factors, window, 0, keepdims=False)
        window_rows = lax.dynamic_slice_in_dim(band_rows, offset_row, WIN, 0)
        result_rows = jnp.dot(
            factor_now.T,
            window_rows,
            precision=lax.Precision.HIGHEST,
            preferred_element_type=jnp.float32,
        )
        return lax.dynamic_update_slice_in_dim(band_rows, result_rows, offset_row, 0)

    def right_step(window, band_cols):
        offset_col = starts[window] - starts[0]
        factor_now = lax.dynamic_index_in_dim(all_factors, window, 0, keepdims=False)
        window_cols = lax.dynamic_slice_in_dim(band_cols, offset_col, WIN, 1)
        result_cols = jnp.dot(
            window_cols,
            factor_now,
            precision=lax.Precision.HIGHEST,
            preferred_element_type=jnp.float32,
        )
        return lax.dynamic_update_slice_in_dim(band_cols, result_cols, offset_col, 1)

    local_tiles = matrix.reshape(row_cycles, tile_size, col_cycles * tile_size)
    rows_each = -(-span_tiles // row_count)
    row_valid, row_index = pick_tiles(first_tile, rows_each, row_count, row_place, span_tiles)
    picked = jnp.where(row_valid[:, None, None], jnp.take(local_tiles, row_index, axis=0), 0.0)
    received = lax.all_to_all(picked, "row", split_axis=2, concat_axis=0, tiled=True)
    band_rows = jnp.take(received, band_order(first_tile, row_count, rows_each, span_tiles), axis=0)
    band_rows = band_rows.reshape(span_tiles * tile_size, received.shape[2])
    band_rows = lax.fori_loop(0, WINS, left_step, band_rows)
    row_tiles = band_rows.reshape(span_tiles, tile_size, received.shape[2])
    send_valid, send_place = slot_order(first_tile, row_count, rows_each, span_tiles)
    backsend = jnp.where(send_valid[:, None, None], jnp.take(row_tiles, send_place, axis=0), 0.0)
    returned = lax.all_to_all(backsend, "row", split_axis=0, concat_axis=2, tiled=True)
    for member in range(rows_each):
        local_tiles = jnp.where(
            row_valid[member],
            lax.dynamic_update_index_in_dim(local_tiles, returned[member], row_index[member], 0),
            local_tiles,
        )
    local_rows = row_cycles * tile_size
    column_view = local_tiles.reshape(local_rows, col_cycles, tile_size)
    cols_each = -(-span_tiles // col_count)
    col_valid, col_index = pick_tiles(first_tile, cols_each, col_count, col_place, span_tiles)
    picked_cols = jnp.where(col_valid[None, :, None], jnp.take(column_view, col_index, axis=1), 0.0)
    col_order = band_order(first_tile, col_count, cols_each, span_tiles)
    gathered = lax.all_gather(picked_cols, "col", axis=1, tiled=True)
    band_cols = jnp.take(gathered, col_order, axis=1).reshape(local_rows, span_tiles * tile_size)
    band_cols = lax.fori_loop(0, WINS, right_step, band_cols)
    own_places = (
        jnp.remainder(col_place - first_tile, col_count)
        + jnp.arange(cols_each, dtype=jnp.int32) * col_count
    )
    own_places = jnp.where(col_valid, own_places, 0)
    returned_cols = jnp.take(
        band_cols.reshape(local_rows, span_tiles, tile_size), own_places, axis=1
    )
    member = 0
    column_view = jnp.where(
        col_valid[member],
        lax.dynamic_update_index_in_dim(
            column_view, returned_cols[:, member], col_index[member], 1
        ),
        column_view,
    )
    return column_view.reshape(matrix.shape)


def solution(mesh):
    placed = (P(None, "row", None, None, "col", None), P(None, None, "col"), P())
    return jax.shard_map(
        body,
        mesh=mesh,
        in_specs=placed,
        out_specs=P(None, "row", None, None, "col", None),
        check_vma=False,
    )
```

profile of v0, /device:TPU:1, one launch (start us, length us, event | category | flops | bytes accessed | tf_op | source)
XLA Modules:
  0.0 615.0 jit_solution(2616811414107815150)
XLA Ops:
  10.4 19.2 %reduce.3 = f32[3,128,32,128]{3,2,1,0:T(8,128)} reduce(f32[3,1,128,32,1,128]{5,4,3,2,1,0:T(1,128)} %param.7, f32[]{:T(128)} %broadcast.920), dimensions={1,4}, to_apply=%param.7.reduce_sub_computation.3 | reduce | bytes 12582916 | tf_op args[0]
  29.6 7.2 %reshape.444 = f32[3,128,4096]{2,1,0:T(8,128)} reshape(f32[3,128,32,128]{3,2,1,0:T(8,128)} %reduce.3) | data formatting | bytes 12582912 | tf_op jit(solution)/shard_map/reshape | solution.py:72
  36.9 6.5 %gather_fusion = f32[3,128,4096]{2,1,0:T(8,128)} fusion(f32[3,128,4096]{2,1,0:T(8,128)} %reshape.444, s32[1024]{0:T(1024)S(1)} %pad_clamp_fusion.3), kind=kCustom, calls=%fused_computation | custom fusion | bytes 12582924 | tf_op jit(solution)/shard_map/jit(_take)/gather | solution.py:75
  43.5 6.8 %select_select_fusion.1 = f32[3,128,4096]{2,1,0:T(8,128)} fusion(f32[3,128,4096]{2,1,0:T(8,128)} %gather_fusion, pred[3]{0:T(512)(128)(4,1)S(1)} %get-tuple-element.227, pred[3]{0:T(512)(128)(4,1)S(1)} %get-tuple-element.244), kind=kLoop, calls=%fused_computation.15 | loop fusion | flops 3145728 | bytes 12582918 | tf_op jit(solution)/shard_map/jit(_where)/select_n | solution.py:75
  50.2 9.2 %copy.53 = f32[3,128,4096]{1,0,2:T(4,128)} copy(f32[3,128,4096]{2,1,0:T(8,128)} %select_select_fusion.1) | data formatting | bytes 12582912 | tf_op jit(solution)/shard_map/jit(_where)/select_n | solution.py:75
  59.5 7.5 %all-to-all-start = ((f32[3,128,4096]{1,0,2:T(4,128)}), f32[3,128,4096]{1,0,2:T(4,128)}, u32[]{:S(2)}, u32[]{:S(2)}) async-start(f32[3,128,4096]{1,0,2:T(4,128)} %copy.53), calls=%async_computation | async-start | bytes 16777216 | tf_op jit(solution)/shard_map/all_to_all | solution.py:76
  67.2 115.0 %all-to-all-done = f32[3,128,4096]{1,0,2:T(4,128)} async-done(((f32[3,128,4096]{1,0,2:T(4,128)}), f32[3,128,4096]{1,0,2:T(4,128)}, u32[]{:S(2)}, u32[]{:S(2)}) %all-to-all-start) | async-done | bytes 6291488 | tf_op jit(solution)/shard_map/all_to_all | solution.py:76
  182.2 6.5 %copy.54 = f32[3,128,4096]{1,2,0:T(8,128)} copy(f32[3,128,4096]{1,0,2:T(4,128)} %all-to-all-done) | data formatting | bytes 12582912 | tf_op jit(solution)/shard_map/all_to_all | solution.py:76
  188.7 6.6 %copy.55 = f32[8,3,128,512]{3,2,1,0:T(8,128)} copy(f32[8,3,128,512]{2,3,0,1:T(8,128)} %bitcast.80) | data formatting | bytes 12582912 | tf_op jit(solution)/shard_map/all_to_all | solution.py:76
  195.3 6.2 %gather_fusion.1 = f32[22,128,512]{2,1,0:T(8,128)} fusion(f32[24,128,512]{2,1,0:T(8,128)} %bitcast.81, s32[1024]{0:T(1024)S(1)} %pad_clamp_fusion.2), kind=kCustom, calls=%fused_computation.1 | custom fusion | bytes 11534424 | tf_op jit(solution)/shard_map/jit(_take)/gather | solution.py:77
  201.5 5.0 bitcast_select_fusion
  206.6 11.3 %copy.56 = f32[10,512,512]{2,1,0:T(8,128)} copy(f32[10,512,512]{1,2,0:T(8,128)} %all-gather.3.cloned.1.call-done) | data formatting | bytes 20971520 | tf_op jit(solution)/shard_map/while | solution.py:79
  217.9 92.9 %while.28 = (s32[]{:T(128)}, f32[2816,512]{1,0:T(8,128)}, f32[10,512,512]{2,1,0:T(8,128)}, s32[10]{0:T(128)S(1)}, s32[]{:T(128)}, /*index=5*/s32[]{:T(128)}, s32[]{:T(128)}) while((s32[]{:T(128)}, f32[2816,512]{1,0:T(8,128)}, f32[10,512,512]{2,1,0:T(8,128)}, s32[10]{0:T(128)S(1)}, s32[]{:T(128)}, /*index=5*/s32[]{:T(128)}, s32[]{:T(128)}) %tuple.93), condition=%wide.region_1.2_spmd, body=%wide.region_0.1_spmd.sunk | while | flops 1610612736 | bytes 5243543 | solution.py:79
  223.1 4.1 dynamic_update_slice.22
  232.4 4.1 dynamic_update_slice.22
  241.8 4.2 dynamic_update_slice.22
  251.1 4.2 dynamic_update_slice.22
  260.5 4.1 dynamic_update_slice.22
  269.8 4.2 dynamic_update_slice.22
  279.1 4.1 dynamic_update_slice.22
  288.5 4.2 dynamic_update_slice.22
  297.9 4.1 dynamic_update_slice.22
  310.8 6.3 %gather_fusion.2 = f32[24,128,512]{2,1,0:T(8,128)} fusion(f32[22,128,512]{2,1,0:T(8,128)} %bitcast.79, s32[1024]{0:T(1024)S(1)} %pad_clamp_fusion.1), kind=kCustom, calls=%fused_computation.2 | custom fusion | bytes 12583008 | tf_op jit(solution)/shard_map/jit(_take)/gather | solution.py:82
  317.0 6.8 %select_select_fusion = f32[24,128,512]{2,1,0:T(8,128)} fusion(f32[24,128,512]{2,1,0:T(8,128)} %gather_fusion.2, pred[24]{0:T(512)(128)(4,1)S(1)} %get-tuple-element.242, pred[24]{0:T(512)(128)(4,1)S(1)} %get-tuple-element.243), kind=kLoop, calls=%fused_computation.14 | loop fusion | flops 3145728 | bytes 12582960 | tf_op jit(solution)/shard_map/jit(_where)/select_n | solution.py:82
  323.9 4.8 all-to-all-start.1
  336.2 78.9 %all-to-all-done.1 = f32[24,128,512]{2,1,0:T(8,128)} async-done(((f32[24,128,512]{2,1,0:T(8,128)}), f32[24,128,512]{2,1,0:T(8,128)}, u32[]{:S(2)}, u32[]{:S(2)}) %all-to-all-start.1) | async-done | bytes 6291488 | tf_op jit(solution)/shard_map/all_to_all | solution.py:83
  429.6 72.6 %all-gather.5.cloned.1.call-done = f32[384,32,128]{2,0,1:T(8,128)} async-done(((f32[384,1,128]{2,0,1:T(8,128)}), f32[384,32,128]{2,0,1:T(8,128)}) %all-gather.5.cloned.1.call-update) | async-done | bytes 6291472 | tf_op jit(solution)/shard_map/all_gather | solution.py:96
  502.2 5.6 gather_fusion.3
  507.8 5.9 copy.61
  513.7 4.4 bitcast_select_fusion.1
  518.1 81.0 %while.29 = (s32[]{:T(128)}, f32[384,2816]{0,1:T(8,128)}, s32[10]{0:T(128)S(1)}, f32[10,512,512]{2,1,0:T(8,128)}, s32[]{:T(128)}, /*index=5*/s32[]{:T(128)}, s32[]{:T(128)}) while((s32[]{:T(128)}, f32[384,2816]{0,1:T(8,128)}, s32[10]{0:T(128)S(1)}, f32[10,512,512]{2,1,0:T(8,128)}, s32[]{:T(128)}, /*index=5*/s32[]{:T(128)}, s32[]{:T(128)}) %tuple.94), condition=%wide.region_3.4_spmd, body=%wide.region_2.3_spmd.sunk | while | flops 1207959552 | bytes 4194967 | solution.py:98
  601.8 6.4 %select_n.478 = f32[384,32,128]{2,1,0:T(8,128)} dynamic-update-slice(f32[384,32,128]{2,1,0:T(8,128)} %bitcast.89, f32[384,1,128]{2,1,0:T(1,128)S(1)} %broadcast_select_fusion.3, s32[]{:T(128)} %constant.284.clone.1, s32[]{:T(128)S(6)} %select_n.475, s32[]{:T(128)} %constant.284.clone.1) | dynamic-update-slice | bytes 393220 | tf_op jit(solution)/shard_map/jit(_where)/select_n | solution.py:108
  (94 shorter events, 132.0 us)
Async XLA Ops:
  6.5 200.0 %all-gather.3.cloned.1.call-start = ((), (), s32[]{:S(2)}) async-start(), calls=%async_computation.2 | async-start | bytes 10813440 | tf_op jit(solution)/shard_map/all_gather | solution.py:46
  59.5 122.7 %all-to-all-start = ((f32[3,128,4096]{1,0,2:T(4,128)}), f32[3,128,4096]{1,0,2:T(4,128)}, u32[]{:S(2)}, u32[]{:S(2)}) async-start(f32[3,128,4096]{1,0,2:T(4,128)} %copy.53), calls=%async_computation | async-start | bytes 16777216 | tf_op jit(solution)/shard_map/all_to_all | solution.py:76
  206.6 11.3 %copy-start.1 = (s32[10]{0:T(128)S(1)}, s32[10]{0:T(128)}, u32[]{:S(2)}) copy-start(s32[10]{0:T(128)} %param.9) | copy-start | bytes 124
  323.9 91.2 %all-to-all-start.1 = ((f32[24,128,512]{2,1,0:T(8,128)}), f32[24,128,512]{2,1,0:T(8,128)}, u32[]{:S(2)}, u32[]{:S(2)}) async-start(f32[24,128,512]{2,1,0:T(8,128)} %select_select_fusion), calls=%async_computation.1 | async-start | bytes 12582912 | tf_op jit(solution)/shard_map/all_to_all | solution.py:83
  328.6 173.6 %all-gather.5.cloned.1.call-start = ((), (), s32[]{:S(2)}) async-start(), calls=%async_computation.3 | async-start | bytes 6488064 | tf_op jit(solution)/shard_map/all_gather | solution.py:96
  418.7 2.2 slice-start
  418.9 2.7 slice-start.1
  425.9 2.7 copy-start
Sparse Core Ops, SparseCore 0:
  9.2 159.0 all-gather.2
  429.6 72.5 all-gather.4
where the time goes:
time: 619 us; the launch traced here: 615 us
  waiting for transfers between devices  267 us (43%)
  local copies, waits for them, and re-layouts  173 us (28%)
  matrix products  67.9 us (11%)
  other arithmetic  47.9 us (8%)
  loops' own time  24.7 us (4%)
  between operations  22.2 us (4%)
  starting transfers between devices  12.5 us (2%)
    all_to_all x1, waiting for transfers between devices, body(): lax.all_to_all(picked, 'row', split_axis=2, concat_axis=0, tiled=True)  115 us
    all_to_all x1, waiting for transfers between devices, body(): lax.all_to_all(backsend, 'row', split_axis=0, concat_axis=2, tiled=True)  78.9 us
    all_gather x1, waiting for transfers between devices, body(): gathered = lax.all_gather(picked_cols, 'col', axis=1, tiled=True)  72.6 us
    dynamic_update_slice x10, local copies, waits for them, and re-layouts, left_step(): lax.dynamic_update_slice_in_dim(band_rows, result_rows, offset_row, 0)  40.8 us
    dot_general x10, matrix products, left_step(): jnp.dot(factor_now.T, window_rows, precision=lax.Precision.HIGHEST, prefe...  34.4 us
    dynamic_update_slice x10, matrix products, right_step(): lax.dynamic_update_slice_in_dim(band_cols, result_cols, offset_col, 1)  33.5 us
    dynamic_update_slice x10, local copies, waits for them, and re-layouts, right_step(): lax.dynamic_update_slice_in_dim(band_cols, result_cols, offset_col, 1)  28.8 us
    unnamed x2, other arithmetic  19.2 us
  transfers between devices with their start and end apart: 4, of which 3 were waited for; matrix products, arithmetic and copies ran while one was open for 12% of the time, Pallas kernels for 0%

commit v1 on v0

v1 whole, which is shorter than its diff:
```python
import functools

import jax
import jax.numpy as jnp
from jax import lax
from jax.experimental import pallas as pl
from jax.experimental.pallas import tpu as pltpu
from jax.sharding import PartitionSpec as P

MESH = pl.DeviceIdType.MESH
NB = 128
WIN = 512
WINS = 10
SPAN = 22
GROUPS = 5
ROWP = 8
COLP = 32
HELD = 4
DEPTH = 3
PEERS = ((0, 1), (1, 0), (2, 1), (3, 0), (1, 1), (2, 0), (3, 1))


def when(condition, action):
    if isinstance(condition, bool):
        if condition:
            action()
    else:
        pl.when(condition)(action)


def both(*conditions):
    result = True
    for condition in conditions:
        if condition is True:
            continue
        if condition is False:
            return False
        result = condition if result is True else jnp.logical_and(result, condition)
    return result


def split(value):
    high = value.astype(jnp.bfloat16)
    low = (value - high.astype(jnp.float32)).astype(jnp.bfloat16)
    return high, low


def dot(a, b):
    return jnp.dot(a, b, preferred_element_type=jnp.float32)


def dot_t(a, b):
    return lax.dot_general(a, b, (((1,), (1,)), ((), ())), preferred_element_type=jnp.float32)


def kernel(first, m, qt, o, band, qf, qh, ql, xh, xl, rbuf, cbuf,
           out_s, out_r, back_s, back_r, own_s, bown_s, rest_s,
           loc_s, y_s, y_r, zp_s, zp_r, zm_s, zm_r, c_s, c_r,
           rr_s, rr_r, rt_s, rt_r, c0_s, c0_r, cb_s, cb_r):
    p = lax.axis_index("row")
    q = lax.axis_index("col")
    x, yh = p // 2, p % 2
    z, yl, core = q // 4, (q // 2) % 2, q % 2

    dsts = [((x + dx) % 4) * 2 + (yh + dy) % 2 for dx, dy in PEERS]
    srcs = [((x + 4 - dx) % 4) * 2 + (yh + dy) % 2 for dx, dy in PEERS]

    def remote(src, dst, ss, rs, row, col):
        return pltpu.make_async_remote_copy(
            src, dst, ss, rs, device_id={"row": row, "col": col}, device_id_type=MESH
        )

    def local(src, dst, s):
        return pltpu.make_async_copy(src, dst, s)

    def in_band(r, s):
        tile = r * 8 + s
        if isinstance(tile, int):
            return first <= tile < first + SPAN
        if isinstance(r, int):
            return True if r == 1 else tile >= first if r == 0 else tile < first + SPAN
        return jnp.logical_and(tile >= first, tile < first + SPAN)

    def rows(tile):
        return pl.ds(pl.multiple_of(tile * NB, NB), NB)

    barrier = pltpu.get_barrier_semaphore()
    for d in dsts:
        pl.semaphore_signal(barrier, inc=1, device_id={"row": d, "col": q}, device_id_type=MESH)

    @pl.loop(1, COLP)
    def _(u):
        pl.semaphore_signal(
            barrier, inc=1, device_id={"row": p, "col": (q + u) % COLP}, device_id_type=MESH
        )

    pl.semaphore_wait(barrier, len(PEERS) + COLP - 1)

    mine = jnp.logical_and(q >= first, q < first + SPAN)

    def col_in(s):
        return jnp.logical_and(s >= first, s < first + SPAN)

    def right_send(u):
        to = (q + u) % COLP
        return remote(
            m.at[:, pl.ds(4 * to, 4), 0, 0], rbuf.at[q, pl.ds(0, 3)], rr_s.at[1], rr_r.at[0], p, to
        )

    def right_own():
        return local(m.at[:, pl.ds(4 * q, 4), 0, 0], rbuf.at[q, pl.ds(0, 3)], rr_s.at[0])

    def right_received(count):
        ref = rbuf.at[pl.ds(0, count), pl.ds(0, 3)]
        remote(ref, ref, rr_s.at[1], rr_r.at[0], dsts[0], q).wait_recv()

    def right_back(u):
        to = (q + u) % COLP
        return remote(
            rbuf.at[to, pl.ds(0, 3)], cbuf.at[:, pl.ds(4 * q, 4), 0], rt_s.at[1], rt_r.at[0], p, to
        )

    def right_back_own():
        return local(rbuf.at[q, pl.ds(0, 3)], cbuf.at[:, pl.ds(4 * q, 4), 0], rt_s.at[0])

    def cols_plain():
        return local(m.at[:, :, 0], cbuf, rt_s.at[0])

    def pair(g, zz, which, n=2, at=0):
        return qf.at[pl.ds(2 * g + at, n), zz, which]

    def own_share(g):
        return local(qt.at[pl.ds(2 * g, 2)], qf.at[pl.ds(2 * g, 2), z, core, yl], loc_s.at[g])

    def y_share(g):
        return remote(
            qt.at[pl.ds(2 * g, 2)], qf.at[pl.ds(2 * g, 2), z, core, yl], y_s.at[0], y_r.at[g],
            p, z * 4 + (1 - yl) * 2 + core,
        )

    def plus(g, j, zz):
        ref = pair(g, zz, core) if j < 3 else pair(g, zz, core, 1, 0)
        return remote(ref, ref, zp_s.at[0], zp_r.at[g, j], p, ((z + 1) % 8) * 4 + yl * 2 + core)

    def minus(g, j, zz):
        ref = pair(g, zz, core) if j < 3 else pair(g, zz, core, 1, 1)
        return remote(ref, ref, zm_s.at[0], zm_r.at[g, j], p, ((z + 7) % 8) * 4 + yl * 2 + core)

    def across(g, b, zz):
        ref = pair(g, zz, core)
        return remote(ref, ref, c_s.at[0], c_r.at[g], p, z * 4 + yl * 2 + 1 - core)

    block_z = [z, (z + 7) % 8, (z + 6) % 8, (z + 5) % 8, (z + 1) % 8, (z + 2) % 8, (z + 3) % 8, (z + 4) % 8]

    def out_copy(r, h, k):
        d = dsts[k]
        return remote(
            m.at[r, :, 4 * d + h, 0], band.at[h, rows(r * 8 + p)], out_s.at[r, h], out_r.at[r], d, q
        )

    def own_copy(r, h):
        return local(m.at[r, :, 4 * p + h, 0], band.at[h, rows(r * 8 + p)], own_s.at[r])

    def held(h, who):
        return jnp.logical_not(jnp.logical_and(h == 0, who == 0))

    def out_batch(i):
        r, h = i // HELD, i % HELD

        @pl.when(i >= DEPTH)
        def _():
            out_sent(i - DEPTH)

        for k, d in enumerate(dsts):
            when(both(in_band(r, p), held(h, d)), lambda k=k: out_copy(r, h, k).start())
        when(both(in_band(r, p), held(h, p)), lambda: own_copy(r, h).start())

    def tiles_ref(slots, count):
        return band.at[pl.ds(0, slots), pl.ds(0, count * NB)]

    def await_sent(slots, count, sem):
        ref = tiles_ref(slots, count)
        remote(ref, ref, sem, out_r.at[0], dsts[0], q).wait_send()

    def await_received(slots, count, sem):
        ref = tiles_ref(slots, count)
        remote(ref, ref, out_s.at[0, 0], sem, dsts[0], q).wait_recv()

    def per_peer(r, action):
        valid = sum(in_band(r, s) for s in range(8))
        for slots, which in ((HELD, p != 0), (HELD - 1, p == 0)):
            when(both(which, in_band(r, p)), lambda slots=slots: action(slots, valid - 1))
            if r != 1:
                when(
                    both(which, jnp.logical_not(in_band(r, p))),
                    lambda slots=slots: action(slots, valid),
                )

    def own_wait(r, sem):
        for slots, which in ((HELD, p != 0), (HELD - 1, p == 0)):
            ref = tiles_ref(slots, 1)
            when(both(which, in_band(r, p)), lambda ref=ref: local(ref, ref, sem).wait())

    def out_wait(r):
        per_peer(r, lambda slots, count: await_received(slots, count, out_r.at[r]))
        own_wait(r, own_s.at[r])

    def out_sent(i):
        r, h = i // HELD, i % HELD
        fewer = jnp.logical_and(h == 0, p != 0)
        when(both(in_band(r, p), fewer), lambda: await_sent(1, 6, out_s.at[r, h]))
        when(both(in_band(r, p), jnp.logical_not(fewer)), lambda: await_sent(1, 7, out_s.at[r, h]))

    def back_copy(r, h, k):
        d = dsts[k]
        return remote(
            band.at[h, rows(r * 8 + d)], o.at[r, :, 4 * p + h, 0], back_s.at[r], back_r.at[r], d, q
        )

    def back_own(r, h):
        return local(band.at[h, rows(r * 8 + p)], o.at[r, :, 4 * p + h, 0], bown_s.at[r])

    def back_send(r):
        @pl.loop(0, HELD)
        def _(h):
            for k, d in enumerate(dsts):
                when(both(in_band(r, d), held(h, p)), lambda k=k: back_copy(r, h, k).start())
            when(both(in_band(r, p), held(h, p)), lambda: back_own(r, h).start())

    def back_wait(r):
        per_peer(r, lambda slots, count: await_sent(slots, count, back_s.at[r]))
        own_wait(r, bown_s.at[r])
        when(both(in_band(r, p), p == 0), lambda: await_received(4, 7, back_r.at[r]))
        when(both(in_band(r, p), p != 0), lambda: await_received(3, 9, back_r.at[r]))

    def rest_copy(r):
        return local(m.at[r, :, pl.ds(1, 31)], o.at[r, :, pl.ds(1, 31)], rest_s.at[r, 0])

    def rest_first(r):
        return local(cbuf.at[r], o.at[r, :, 0], rest_s.at[r, 1])

    def first_out(r):
        return remote(cbuf.at[r, :, 0], band.at[HELD, rows(r * 8 + p)], c0_s.at[r], c0_r.at[r, p], 0, q)

    def first_in(r, s):
        return remote(cbuf.at[r, :, 0], band.at[HELD, rows(r * 8 + s)], c0_s.at[r], c0_r.at[r, s], 0, q)

    def first_own(r):
        return local(cbuf.at[r, :, 0], band.at[HELD, rows(r * 8)], c0_s.at[r])

    def first_back(r, s):
        return remote(band.at[HELD, rows(r * 8 + s)], o.at[r, :, 0, 0], cb_s.at[r, s], cb_r.at[r], s, q)

    def first_back_own(r):
        return local(band.at[HELD, rows(r * 8)], o.at[r, :, 0, 0], cb_s.at[r, 0])

    def convert(w):
        @pl.loop(0, 8)
        def _(zz):
            for a in range(2):
                for b in range(2):
                    at = pl.ds(pl.multiple_of(zz * 64 + b * 32 + a * 16, 16), 16)
                    high, low = split(qf[w, zz, a, b])
                    qh[w, at, :] = high
                    ql[w, at, :] = low

    def left_window(w, h, n):
        base = (first + 2 * w) * NB
        for i in range(n):
            high, low = split(band[h + i, pl.ds(pl.multiple_of(base, NB), WIN), :])
            xh[:, i * NB:(i + 1) * NB] = high
            xl[:, i * NB:(i + 1) * NB] = low
        xhv, xlv = xh[:, : n * NB], xl[:, : n * NB]

        @pl.loop(0, 2)
        def _(part):
            at = pl.ds(pl.multiple_of(part * 256, 256), 256)
            qhv, qlv = qh[w, at, :], ql[w, at, :]
            y = dot(qhv, xhv) + dot(qhv, xlv) + dot(qlv, xhv)
            to = pl.ds(pl.multiple_of(base + part * 256, NB), 256)
            for i in range(n):
                band[h + i, to, :] = y[:, i * NB:(i + 1) * NB]

    flat = rbuf.reshape(24 * 16, NB)

    def right_window(w):
        ats = [pl.ds(pl.multiple_of((first + 2 * w + j) * 16, 16), 16) for j in range(4)]
        value = jnp.concatenate([flat[at, :] for at in ats], axis=1)
        high, low = split(value)
        qhv, qlv = qh[w], ql[w]
        y = dot_t(high, qhv) + dot_t(low, qhv) + dot_t(high, qlv)
        for j, at in enumerate(ats):
            flat[at, :] = y[:, j * NB:(j + 1) * NB]

    when(mine, lambda: right_own().start())

    @pl.when(mine)
    def _():
        @pl.loop(1, COLP)
        def _(u):
            right_send(u).start()

    when(jnp.logical_not(mine), lambda: cols_plain().start())
    for g in range(GROUPS):
        y_share(g).start()
        own_share(g).start()

    @pl.loop(0, DEPTH)
    def _(i):
        out_batch(i)

    @pl.when(p == 0)
    def _():
        band[0] = jnp.zeros_like(band[0])

    @pl.loop(0, GROUPS)
    def _(g):
        own_share(g).wait()
        y_share(g).wait_recv()
        plus(g, 0, z).start()
        minus(g, 0, z).start()
        across(g, 0, z).start()

    for r in (0, 2):
        when(jnp.logical_not(in_band(r, p)), lambda r=r: rest_copy(r).start())

    for j in range(4):
        @pl.loop(0, GROUPS)
        def _(g, j=j):
            event = j * GROUPS + g
            plus(g, j, (z + 7 - j) % 8).wait_recv()
            if j < 3:
                plus(g, j + 1, (z + 7 - j) % 8).start()
                across(g, 1 + j, block_z[1 + j]).start()
            minus(g, j, (z + 1 + j) % 8).wait_recv()
            if j < 3:
                minus(g, j + 1, (z + 1 + j) % 8).start()
                across(g, 4 + j, block_z[4 + j]).start()
            else:
                across(g, 7, block_z[7]).start()

            @pl.when(jnp.logical_and(event % 2 == 0, event < 2 * (3 * HELD - DEPTH)))
            def _():
                out_batch(DEPTH + event // 2)

            if j == 3:
                theirs = qf.at[pl.ds(2 * g, 2), :, 1 - core]
                remote(theirs, theirs, c_s.at[0], c_r.at[g], dsts[0], q).wait_recv()

                @pl.when(g == 0)
                def _():
                    when(mine, lambda: right_own().wait())

                    when(mine, lambda: right_received(SPAN - 1))
                    when(jnp.logical_not(mine), lambda: right_received(SPAN))

                @pl.loop(2 * g, 2 * g + 2)
                def _(w):
                    convert(w)
                    right_window(w)

    @pl.loop(1, COLP)
    def _(u):
        when(col_in((q + u) % COLP), lambda: right_back(u).start())

    when(mine, lambda: right_back_own().start())
    needs = [[w for w in range(WINS) if (first + 2 * w + 3) // 8 >= r][0] for r in range(3)]

    @pl.loop(0, WINS)
    def _(w):
        @pl.when(w == needs[0])
        def _():
            out_wait(0)

        @pl.when(w == needs[1])
        def _():
            out_wait(1)

        @pl.when(w == needs[2])
        def _():
            when(mine, lambda: right_back_own().wait())
            when(jnp.logical_not(mine), lambda: cols_plain().wait())

            ref = cbuf.at[:, pl.ds(0, 4 * (COLP - 1))]
            when(mine, lambda: remote(ref, ref, rt_s.at[1], rt_r.at[0], dsts[0], q).wait_recv())

            for r in range(3):
                when(both(in_band(r, p), p != 0), lambda r=r: first_out(r).start())
                when(both(in_band(r, p), p == 0), lambda r=r: first_own(r).start())
                if r != 1:
                    when(jnp.logical_not(in_band(r, p)), lambda r=r: rest_first(r).start())
            out_wait(2)

        @pl.loop(0, 2)
        def _(pr):
            left_window(w, pr * 2, 2)

        @pl.when(w % 2 == 1)
        def _():
            @pl.when(w == 3)
            def _():
                back_send(0)

            @pl.when(w == 7)
            def _():
                back_send(1)

            @pl.when(w == 9)
            def _():
                back_send(2)

    @pl.when(p == 0)
    def _():
        for r in range(3):
            when(in_band(r, p), lambda r=r: first_own(r).wait())
            for s in range(1, 8):
                if in_band(r, s):
                    first_in(r, s).wait_recv()

        @pl.loop(0, WINS)
        def _(w):
            left_window(w, HELD, 1)

        for r in range(3):
            when(in_band(r, p), lambda r=r: first_back_own(r).start())
            for s in range(1, 8):
                if in_band(r, s):
                    first_back(r, s).start()

    def right_returned(count):
        ref = rbuf.at[pl.ds(0, count), pl.ds(0, 3)]
        remote(ref, ref, rt_s.at[1], rt_r.at[0], dsts[0], q).wait_send()

    sent = cbuf.at[:, pl.ds(0, 4 * (COLP - 1))]
    when(mine, lambda: remote(sent, sent, rr_s.at[1], rr_r.at[0], dsts[0], q).wait_send())
    when(mine, lambda: right_returned(SPAN - 1))
    when(jnp.logical_not(mine), lambda: right_returned(SPAN))

    for ref, sem, got in (
        (qf.at[:, z, core, yl], y_s, y_r),
        (qf.at[pl.ds(0, GROUPS), pl.ds(0, 7), core], zp_s, c_r),
        (qf.at[pl.ds(0, GROUPS), pl.ds(0, 7), core], zm_s, c_r),
        (qf.at[:, :, core], c_s, c_r),
    ):
        remote(ref, ref, sem.at[0], got.at[0], dsts[0], q).wait_send()

    @pl.loop(3 * HELD - DEPTH, 3 * HELD)
    def _(i):
        out_sent(i)

    for r in range(3):
        back_wait(r)
        when(both(in_band(r, p), p != 0), lambda r=r: first_out(r).wait_send())
        when(both(in_band(r, p), p != 0), lambda r=r: first_back(r, p).wait_recv())
        if r != 1:
            when(jnp.logical_not(in_band(r, p)), lambda r=r: rest_copy(r).wait())
            when(jnp.logical_not(in_band(r, p)), lambda r=r: rest_first(r).wait())

    @pl.when(p == 0)
    def _():
        for r in range(3):
            when(in_band(r, p), lambda r=r: first_back_own(r).wait())
            for s in range(1, 8):
                if in_band(r, s):
                    first_back(r, s).wait_send()


def update(first, tiles, shares):
    dma = pltpu.SemaphoreType.DMA
    return pl.pallas_call(
        functools.partial(kernel, first),
        out_shape=jax.ShapeDtypeStruct(tiles.shape, tiles.dtype),
        in_specs=[pl.BlockSpec(memory_space=pl.ANY)] * 2,
        out_specs=pl.BlockSpec(memory_space=pl.ANY),
        scratch_shapes=[
            pltpu.VMEM((HELD + 1, 24 * NB, NB), jnp.float32),
            pltpu.VMEM((WINS, 8, 2, 2, 16, WIN), jnp.float32),
            pltpu.VMEM((WINS, WIN, WIN), jnp.bfloat16),
            pltpu.VMEM((WINS, WIN, WIN), jnp.bfloat16),
            pltpu.VMEM((WIN, 2 * NB), jnp.bfloat16),
            pltpu.VMEM((WIN, 2 * NB), jnp.bfloat16),
            pltpu.VMEM((24, 4, 4, NB), jnp.float32),
            pltpu.VMEM((3, NB, 1, NB), jnp.float32),
            dma((3, HELD)), dma((3,)), dma((3,)), dma((3,)), dma((3,)), dma((3,)), dma((3, 2)),
            dma((GROUPS,)), dma((1,)), dma((GROUPS,)),
            dma((1,)), dma((GROUPS, 4)), dma((1,)), dma((GROUPS, 4)),
            dma((1,)), dma((GROUPS,)),
            dma((2,)), dma((1,)), dma((2,)), dma((1,)),
            dma((3,)), dma((3, ROWP)), dma((3, ROWP)), dma((3,)),
        ],
        compiler_params=pltpu.CompilerParams(
            collective_id=first, has_side_effects=True, vmem_limit_bytes=50 * 2**20
        ),
        cost_estimate=pl.CostEstimate(flops=8 * 10**9, bytes_accessed=20 * 10**6, transcendentals=0),
        name=f"sweep{first}",
    )(tiles, shares)


def body(matrix, factors, starts):
    tiles = matrix.reshape(3, NB, COLP, 1, NB)
    shares = jnp.transpose(factors, (0, 2, 1))
    updated = lax.switch(
        starts[0] // NB, [functools.partial(update, first) for first in range(3)], tiles, shares
    )
    return updated.reshape(matrix.shape)


def solution(mesh):
    placed = (P(None, "row", None, None, "col", None), P(None, None, "col"), P())
    return jax.shard_map(
        body,
        mesh=mesh,
        in_specs=placed,
        out_specs=P(None, "row", None, None, "col", None),
        check_vma=False,
    )
```

time: 619 us -> 174 us (0.28)
  waiting for transfers between devices: 267 us -> 0 us
  local copies, waits for them, and re-layouts: 173 us -> 2.71 us
  Pallas kernels: 0 us -> 168 us
  matrix products: 67.9 us -> 0 us
  other arithmetic: 47.9 us -> 0 us
  loops' own time: 24.7 us -> 0.03 us
  between operations: 22.2 us -> 2.62 us
  starting transfers between devices: 12.5 us -> 0 us
    all_to_all x2 -> x0, waiting for transfers between devices: 194 us -> none  [the longest x1 115 us: body(): lax.all_to_all(picked, 'row', split_axis=2, concat_axis=0, tiled=True)]
    pallas_call x0 -> x1, Pallas kernels: none -> 168 us  [update(): pl.pallas_call(functools.partial(kernel, first), out_shape=jax.ShapeDtype...]
    all_gather x2 -> x0, waiting for transfers between devices: 72.6 us -> none  [the longest x1 72.6 us: body(): gathered = lax.all_gather(picked_cols, 'col', axis=1, tiled=True)]
    dynamic_update_slice x20 -> x0, local copies, waits for them, and re-layouts: 69.6 us -> none  [the longest x10 40.8 us: left_step(): lax.dynamic_update_slice_in_dim(band_rows, result_rows, offset_row, 0)]
    dot_general x10 -> x0, matrix products: 34.4 us -> none  [left_step(): jnp.dot(factor_now.T, window_rows, precision=lax.Precision.HIGHEST, prefe...]
    dynamic_update_slice x10 -> x0, matrix products: 33.5 us -> none  [right_step(): lax.dynamic_update_slice_in_dim(band_cols, result_cols, offset_col, 1)]
    gather x5 -> x0, local copies, waits for them, and re-layouts: 30.5 us -> none  [the longest x2 11.5 us: body(): jnp.take(gathered, col_order, axis=1)]
    select_n x13 -> x0, other arithmetic: 28.6 us -> none  [the longest x1 6.82 us: body(): jnp.where(send_valid[:, None, None], jnp.take(row_tiles, send_place, axis...]
  transfers between devices with their start and end apart: 4 -> 0, of which waited for: 3 -> 0; matrix products, arithmetic and copies ran while one was open for 12% -> 0% of each run, Pallas kernels for 0% -> 0%
where the time goes in v1:
time: 174 us
  Pallas kernels  168 us (97%)
  local copies, waits for them, and re-layouts  2.71 us (2%)
  between operations  2.62 us (2%)
    pallas_call x1, Pallas kernels, update(): pl.pallas_call(functools.partial(kernel, first), out_shape=jax.ShapeDtype...  168 us

profile of v1, /device:TPU:1, one launch (start us, length us, event | category | flops | bytes accessed | tf_op | source)
XLA Modules:
  0.0 173.5 jit_solution(17502135078152095693)
XLA Ops:
  2.6 168.2 %conditional.1 = (f32[3,1,128,32,1,128]{5,4,3,2,1,0:T(1,128)S(1)}) conditional(s32[]{:T(128)} %clamp.3, (f32[3,1,128,32,1,128]{5,4,3,2,1,0:T(1,128)}, f32[10,16,512]{2,1,0:T(8,128)}) %tuple.30, (f32[3,1,128,32,1,128]{5,4,3,2,1,0:T(1,128)}, f32[10,16,512]{2,1,0:T(8,128)}) %tuple.31, (f32[3,1,128,32,1,128]{5,4,3,2,1,0:T(1,128)}, ...), branch_computations={%region_0.1_spmd, %region_1.2_spmd, %region_2.3_spmd} | conditional | flops 8000000000 | bytes 20000008 | solution.py:502
  2.6 168.2 %sweep2.1 = f32[3,128,32,1,128]{4,3,2,1,0:T(1,128)S(1)} custom-call(f32[3,128,32,1,128]{4,3,2,1,0:T(1,128)} %bitcast.30, f32[10,16,512]{2,1,0:T(8,128)} %get-tuple-element.30.qt), custom_call_target="tpu_custom_call" | custom-call | flops 8000000000 | bytes 20000000 | tf_op jit(solution)/shard_map/cond/branch_2_fun/sweep2/pallas_call | solution.py:470
  170.8 2.7 %copy.21 = f32[3,1,128,32,1,128]{5,4,3,2,1,0:T(1,128)} copy(f32[3,1,128,32,1,128]{5,4,3,2,1,0:T(1,128)S(1)} %get-tuple-element.44) | data formatting | bytes 12582912

commit v2 on v1

--- a/solution.py
+++ b/solution.py
@@ -16,7 +16,7 @@
 ROWP = 8
 COLP = 32
 HELD = 4
-DEPTH = 3
+DEPTH = 2
 PEERS = ((0, 1), (1, 0), (2, 1), (3, 0), (1, 1), (2, 0), (3, 1))
 
 
@@ -292,15 +292,6 @@
         for j, at in enumerate(ats):
             flat[at, :] = y[:, j * NB:(j + 1) * NB]
 
-    when(mine, lambda: right_own().start())
-
-    @pl.when(mine)
-    def _():
-        @pl.loop(1, COLP)
-        def _(u):
-            right_send(u).start()
-
-    when(jnp.logical_not(mine), lambda: cols_plain().start())
     for g in range(GROUPS):
         y_share(g).start()
         own_share(g).start()
@@ -320,6 +311,16 @@
         plus(g, 0, z).start()
         minus(g, 0, z).start()
         across(g, 0, z).start()
+
+    when(mine, lambda: right_own().start())
+
+    @pl.when(mine)
+    def _():
+        @pl.loop(1, COLP)
+        def _(u):
+            right_send(u).start()
+
+    when(jnp.logical_not(mine), lambda: cols_plain().start())
 
     for r in (0, 2):
         when(jnp.logical_not(in_band(r, p)), lambda r=r: rest_copy(r).start())

time: 174 us -> 171 us (0.983)
  Pallas kernels: 168 us -> 164 us
    pallas_call x1, Pallas kernels: 168 us -> 164 us  [update(): pl.pallas_call(functools.partial(kernel, first), out_shape=jax.ShapeDtype...]
where the time goes in v2:
time: 171 us; the launch traced here: 170 us
  Pallas kernels  164 us (96%)
  local copies, waits for them, and re-layouts  2.71 us (2%)
  between operations  2.62 us (2%)
    pallas_call x1, Pallas kernels, update(): pl.pallas_call(functools.partial(kernel, first), out_shape=jax.ShapeDtype...  164 us

profile of v2, /device:TPU:1, one launch (start us, length us, event | category | flops | bytes accessed | tf_op | source)
XLA Modules:
  0.0 169.7 jit_solution(16693301555134307365)
XLA Ops:
  2.6 164.4 %conditional.1 = (f32[3,1,128,32,1,128]{5,4,3,2,1,0:T(1,128)S(1)}) conditional(s32[]{:T(128)} %clamp.3, (f32[3,1,128,32,1,128]{5,4,3,2,1,0:T(1,128)}, f32[10,16,512]{2,1,0:T(8,128)}) %tuple.30, (f32[3,1,128,32,1,128]{5,4,3,2,1,0:T(1,128)}, f32[10,16,512]{2,1,0:T(8,128)}) %tuple.31, (f32[3,1,128,32,1,128]{5,4,3,2,1,0:T(1,128)}, ...), branch_computations={%region_0.1_spmd, %region_1.2_spmd, %region_2.3_spmd} | conditional | flops 8000000000 | bytes 20000008 | solution.py:503
  2.6 164.3 %sweep1.1 = f32[3,128,32,1,128]{4,3,2,1,0:T(1,128)S(1)} custom-call(f32[3,128,32,1,128]{4,3,2,1,0:T(1,128)} %bitcast.29, f32[10,16,512]{2,1,0:T(8,128)} %get-tuple-element.28.qt), custom_call_target="tpu_custom_call" | custom-call | flops 8000000000 | bytes 20000000 | tf_op jit(solution)/shard_map/cond/branch_1_fun/sweep1/pallas_call | solution.py:471
  167.0 2.7 %copy.21 = f32[3,1,128,32,1,128]{5,4,3,2,1,0:T(1,128)} copy(f32[3,1,128,32,1,128]{5,4,3,2,1,0:T(1,128)S(1)} %get-tuple-element.44) | data formatting | bytes 12582912
